TPU v7x, 256 devices: a whole 4x4x8 slice. The times are simulated.
256 devices in a mesh: dp: 16 (over z, x_lo), mp: 16 (over x_hi, y, core).
Axes of the slice: x: 4 (x_hi: 2, x_lo: 2; x = x_hi * 2 + x_lo), y: 4, z: 8, core: 2. Of those that a mesh axis runs over, the one named last changes fastest.
Arguments:
- grads: bfloat16 [1024, 1048576], P('dp', 'mp'), as said below
- sign_bits: int32 [1048576], P('mp'), may hold values from 0 to 1
- columns: int32 [8192], replicated, may hold values from 0 to 1048575
Outputs:
- gram: float32 [1024, 1024], P('dp', 'mp')
Inputs may be any that keep to these rules, and one draw needn't show every extreme that they name: `grads`: gradients of different examples share a common direction with example-dependent coefficients, plus independent parts.
All inputs are finite; a program needn't handle non-finite values.
Results may differ from a plain program's by a relative error of at most 0.00041.
Values may be sent and summed in bfloat16 or wider, within the bound.
A program may use at most 128 MiB of HBM per device.

v0:
```python
import jax
import jax.numpy as jnp
from jax import lax
from jax.sharding import PartitionSpec as P

SKETCH = 8192


def parity_of(values, bit_count):
    parity_sum = jnp.zeros_like(values)
    for bit_place in range(bit_count):
        parity_sum = parity_sum + jnp.bitwise_and(jnp.right_shift(values, bit_place), 1)
    return parity_sum % 2


def hadamard(order):
    rows = lax.iota(jnp.int32, order)
    parity = parity_of(
        jnp.bitwise_and(rows[:, None], rows[None, :]), max(order - 1, 1).bit_length()
    )
    return (1 - 2 * parity).astype(jnp.bfloat16)


def per_device(grads, sign_bits, columns):
    rows_here = grads.shape[0]
    block_len = grads.shape[1]
    groups = lax.axis_size("mp")
    level = (block_len.bit_length() - 1) // 2
    size_a = 2**level
    size_b = block_len // size_a
    signs = (2 * sign_bits - 1).astype(jnp.bfloat16)
    signed = (grads * signs[None, :]).reshape(rows_here, size_a, size_b)
    first = jnp.einsum(
        "rab,bc->rac", signed, hadamard(size_b), preferred_element_type=jnp.float32
    ).astype(jnp.bfloat16)
    second = jnp.einsum("rac,ad->rdc", first, hadamard(size_a), preferred_element_type=jnp.float32)
    flat = second.reshape(rows_here, block_len)
    high = columns // block_len
    low = columns % block_len
    scale = 1.0 / jnp.sqrt(jnp.float32(SKETCH))
    mine = lax.axis_index("mp")
    group_bits = max(groups, 2).bit_length()
    parity = parity_of(jnp.bitwise_and(high, mine), group_bits)
    weight = (1 - 2 * parity).astype(jnp.float32)
    terms = flat[:, low] * weight[None, :]
    sketch = (lax.psum_scatter(terms, "mp", scatter_dimension=1, tiled=True) * scale).astype(
        jnp.bfloat16
    )
    partial_gram = lax.dot_general(
        sketch,
        lax.all_gather(sketch, "dp", axis=0, tiled=True),
        (((1,), (1,)), ((), ())),
        preferred_element_type=jnp.float32,
    )
    return lax.psum_scatter(partial_gram, "mp", scatter_dimension=1, tiled=True)


def solution(mesh):
    return jax.shard_map(
        per_device,
        mesh=mesh,
        in_specs=(P("dp", "mp"), P("mp"), P()),
        out_specs=P("dp", "mp"),
        check_vma=False,
    )
```

profile of v0, /device:TPU:7, one launch (start us, length us, event | category | flops | bytes accessed | tf_op | source)
XLA Modules:
  0.0 345.5 jit_solution(13794582628904936319)
XLA Ops:
  6.5 0.0 reduce-scatter.5.cloned.1.call-start
  6.5 1.0 add_convert_fusion
  7.5 8.0 %broadcast_multiply_fusion = bf16[64,65536]{1,0:T(8,128)(2,1)} fusion(bf16[64,65536]{1,0:T(8,128)(2,1)} %param.3, bf16[65536]{0:T(1024)(128)(2,1)S(1)} %add_convert_fusion), kind=kLoop, calls=%fused_computation.5 | loop fusion | flops 4194304 | bytes 16908288 | tf_op jit(solution)/shard_map/mul | solution.py:32
  15.5 8.8 %copy.10 = bf16[8,8,256,256]{3,2,1,0:T(8,128)(2,1)} copy(bf16[8,8,256,256]{3,1,2,0:T(8,128)(2,1)} %bitcast.19) | data formatting | bytes 16777216
  24.4 11.0 %convolution_bitcast_fusion = f32[64,256,256]{2,1,0:T(8,128)} fusion(bf16[64,256,256]{2,1,0:T(8,128)(2,1)} %bitcast.18), kind=kOutput, calls=%fused_computation.1 | convolution fusion | flops 4304142336 | bytes 25165824 | tf_op jit(solution)/shard_map/rac,ad->rdc/dot_general | solution.py:36
  35.4 0.0 copy-start
  35.4 23.1 %copy.7 = f32[64,256,256]{0,2,1:T(8,128)} copy(f32[64,256,256]{2,1,0:T(8,128)} %convolution_bitcast_fusion) | data formatting | bytes 33554432 | tf_op jit(solution)/shard_map/reshape | solution.py:37
  58.5 0.0 copy-done
  58.5 0.1 fusion.30
  58.6 38.3 %gather_fusion = f32[8192,64]{1,0:T(8,128)} fusion(f32[64,65536]{0,1:T(8,128)} %bitcast.17, s32[8192]{0:T(1024)S(1)} %get-tuple-element.6), kind=kCustom, calls=%fused_computation | custom fusion | bytes 4227072 | tf_op jit(solution)/shard_map/gather | solution.py:45
  96.9 4.3 %multiply_bitcast_fusion = f32[64,8192]{0,1:T(8,128)} fusion(f32[8192,64]{1,0:T(8,128)} %gather_fusion, f32[8192]{0:T(1024)S(1)} %get-tuple-element.5), kind=kLoop, calls=%fused_computation.4 | loop fusion | flops 524288 | bytes 4227072 | tf_op jit(solution)/shard_map/mul | solution.py:45
  101.2 0.0 reduce-scatter.5.cloned.1.call-update
  101.2 0.0 all-gather.2.cloned.1.call-start
  101.2 88.7 %reduce-scatter.5.cloned.1.call-done = f32[64,512]{0,1:T(8,128)} async-done(((f32[64,8192]{0,1:T(8,128)}), f32[64,512]{0,1:T(8,128)}) %reduce-scatter.5.cloned.1.call-update) | async-done | bytes 131088 | tf_op jit(solution)/shard_map/reduce_scatter | solution.py:46
  190.0 1.0 multiply_convert_fusion
  190.9 0.7 copy.6
  191.7 0.0 all-gather.2.cloned.1.call-update
  191.7 0.0 reduce-scatter.7.cloned.1.call-start
  191.7 59.6 %all-gather.2.cloned.1.call-done = bf16[1024,512]{1,0:T(8,128)(2,1)} async-done(((bf16[64,512]{1,0:T(8,128)(2,1)}), bf16[1024,512]{1,0:T(8,128)(2,1)}) %all-gather.2.cloned.1.call-update) | async-done | bytes 1048592 | tf_op jit(solution)/shard_map/all_gather | solution.py:51
  251.4 2.5 convolution_bitcast_fusion.1
  253.8 0.0 reduce-scatter.7.cloned.1.call-update
  253.8 83.7 %reduce-scatter.7.cloned.1.call-done = f32[64,64]{1,0:T(8,128)} async-done(((f32[1024,64]{1,0:T(8,128)}), f32[64,64]{1,0:T(8,128)}) %reduce-scatter.7.cloned.1.call-update) | async-done | bytes 16400
  337.5 1.5 copy.9
Async XLA Ops:
  6.5 183.4 %reduce-scatter.5.cloned.1.call-start = ((), (), s32[]{:S(2)}) async-start(), calls=%async_computation.2 | async-start | bytes 4456448 | tf_op jit(solution)/shard_map/reduce_scatter | solution.py:46
  35.4 23.1 %copy-start = (s32[8192]{0:T(1024)S(1)}, s32[8192]{0:T(1024)}, u32[]{:S(2)}) copy-start(s32[8192]{0:T(1024)} %param.5) | copy-start | bytes 98308
  101.2 150.2 %all-gather.2.cloned.1.call-start = ((), (), s32[]{:S(2)}) async-start(), calls=%async_computation.3 | async-start | bytes 1114112 | tf_op jit(solution)/shard_map/all_gather | solution.py:51
  191.7 145.8 %reduce-scatter.7.cloned.1.call-start = ((), (), s32[]{:S(2)}) async-start(), calls=%async_computation.4 | async-start | bytes 557056
Sparse Core Ops, SparseCore 0:
  101.3 88.6 reduce-scatter.4
  191.9 59.4 all-gather.1
  255.9 81.6 reduce-scatter.6
where the time goes:
time: 349 us; the launch traced here: 346 us
  waiting for transfers between devices  232 us (66%)
  local copies, waits for them, and re-layouts  72.5 us (21%)
  other arithmetic  14.3 us (4%)
  matrix products  13.5 us (4%)
  between operations  13.1 us (4%)
    reduce_scatter x1, waiting for transfers between devices, per_device(): lax.psum_scatter(terms, 'mp', scatter_dimension=1, tiled=True) * scale  88.7 us
    unnamed x4, waiting for transfers between devices  83.7 us
    all_gather x1, waiting for transfers between devices, per_device(): lax.all_gather(sketch, 'dp', axis=0, tiled=True)  59.6 us
    gather x1, local copies, waits for them, and re-layouts, per_device(): terms = flat[:, low] * weight[None, :]  38.3 us
    reshape x1, local copies, waits for them, and re-layouts, per_device(): flat = second.reshape(rows_here, block_len)  23.1 us
    dot_general x1, matrix products, per_device(): jnp.einsum('rac,ad->rdc', first, hadamard(size_a), preferred_element_type...  11 us
    unnamed x4, local copies, waits for them, and re-layouts  10.3 us
    mul x1, other arithmetic, per_device(): signed = (grads * signs[None, :]).reshape(rows_here, size_a, size_b)  7.98 us
  transfers between devices with their start and end apart: 3, of which 3 were waited for; matrix products, arithmetic and copies ran while one was open for 0% of the time, Pallas kernels for 0%

commit v1 on v0

v1 whole, which is shorter than its diff:
```python
import functools

import jax
import jax.numpy as jnp
from jax import lax
from jax.experimental import pallas as pl
from jax.experimental.pallas import tpu as pltpu
from jax.sharding import PartitionSpec as P

SKETCH = 8192
ROWS = 64
LOCAL = 65536
CHUNKS = 16
STRIDE = 264


def parity(v, bits):
    p = v & 1
    for i in range(1, bits):
        p = p ^ ((v >> i) & 1)
    return p


def iota(shape, axis):
    return lax.broadcasted_iota(jnp.int32, shape, axis)


def hadamard(order, bits):
    both = iota((order, order), 0) & iota((order, order), 1)
    return (1 - 2 * parity(both, bits)).astype(jnp.float32).astype(jnp.bfloat16)


def local_kernel(
    grads, bits, columns, out, data, sign, cols, rows_v, rows_s, first, second, picked, sa, sb, had_b, had_a, gsem, ssem
):
    copy_sign = pltpu.make_async_copy(bits, sign, ssem.at[0])
    copy_cols = pltpu.make_async_copy(columns, cols, ssem.at[1])
    copy_cols.start()
    copy_sign.start()
    width = LOCAL // CHUNKS

    def chunk(i):
        return pltpu.make_async_copy(grads.at[:, pl.ds(i * width, width)], data.at[i], gsem.at[i])

    for i in range(CHUNKS):
        chunk(i).start()
    had_b[...] = hadamard(256, 8)
    had_a[...] = hadamard(128, 7)
    copy_cols.wait()
    cv = cols[...]
    rows_v[...] = ((cv & 255) << 7) | ((cv & 65535) >> 9)
    copy_rows = pltpu.make_async_copy(rows_v, rows_s, ssem.at[2])
    copy_rows.start()
    me = lax.axis_index("mp")
    eye = iota((128, 128), 0) == iota((128, 128), 1)
    halves = ((iota((256, 128), 0) >> 7) == (iota((256, 128), 1) >> 6)).astype(jnp.float32).astype(jnp.bfloat16)
    w = 1.0 - 2.0 * parity((cv >> 16) & me, 4).astype(jnp.float32)
    ws = w * (1.0 - 2.0 * ((cv >> 8) & 1).astype(jnp.float32))

    def spread(v1, v2):
        d = jnp.concatenate([jnp.where(eye, v1, 0.0), jnp.where(eye, v2, 0.0)], axis=1)
        return jnp.dot(d.astype(jnp.bfloat16), halves, preferred_element_type=jnp.float32)

    for j in range(16):
        for t in range(2):
            p, q = 4 * j + t, 4 * j + 2 + t
            sa[pl.ds(j * 256 + t * 128, 128), :] = spread(w[p : p + 1], ws[q : q + 1])
            sb[pl.ds(j * 256 + t * 128, 128), :] = spread(ws[p : p + 1], w[q : q + 1])
    copy_sign.wait()

    @pl.loop(0, CHUNKS)
    def _(i):
        chunk(i).wait()
        for q in range(4):
            s = (2 * sign[pl.ds(pl.multiple_of(i * 32 + q * 8, 8), 8), :] - 1).astype(jnp.float32).astype(jnp.bfloat16)
            parts = []
            for a in range(4):
                both = []
                for h in range(2):
                    x = data[i, :, pl.ds((q * 4 + a) * 256 + h * 128, 128)]
                    both.append(x * s[2 * a + h : 2 * a + h + 1, :])
                parts.append(jnp.concatenate(both, axis=1))
            block = jnp.concatenate(parts, axis=0)
            o = lax.dot_general(had_b[...], block, (((1,), (1,)), ((), ())), preferred_element_type=jnp.float32)
            g = pl.multiple_of((i * 4 + q) * (2 * STRIDE), 8)
            first[pl.ds(g, 256), :] = o[:, :128]
            first[pl.ds(pl.multiple_of(g + STRIDE, 8), 256), :] = o[:, 128:]

    @pl.loop(0, 32)
    def _(i):
        for q in range(4):
            c = i * 8 + q * 2
            z0 = first[pl.ds(c, 128, stride=STRIDE), :].astype(jnp.bfloat16)
            z1 = first[pl.ds(c + 1, 128, stride=STRIDE), :].astype(jnp.bfloat16)
            o = jnp.dot(had_a[...], jnp.concatenate([z0, z1], axis=1), preferred_element_type=jnp.float32)
            second[pl.ds(pl.multiple_of(c * 128, 128), 128), :] = o[:, :128]
            second[pl.ds(pl.multiple_of(c * 128 + 128, 128), 128), :] = o[:, 128:]

    copy_rows.wait()

    @pl.loop(0, 16)
    def _(j):
        @pl.loop(0, 2)
        def _(u):
            for h in range(2):
                for b in range(8):
                    at = [rows_s[j * 4 + u + 2 * h, b * 16 + e] for e in range(16)]
                    got = [second[pl.ds(r, 1), :] for r in at]
                    for e in range(16):
                        picked[h, pl.ds(u * 128 + b * 16 + e, 1), :] = got[e]

        low = iota((256, 128), 1) < 64
        x = picked[0]
        y = picked[1]
        here = pl.ds(pl.multiple_of(j * 256, 256), 256)
        out[here, :] = (
            jnp.where(low, x, y) * sa[here, :] + pltpu.roll(jnp.where(low, y, x), 64, 1) * sb[here, :]
        )


def local(grads, sign_bits, columns):
    return pl.pallas_call(
        local_kernel,
        out_shape=jax.ShapeDtypeStruct((4096, 128), jnp.float32),
        in_specs=[pl.BlockSpec(memory_space=pl.ANY)] * 3,
        out_specs=pl.BlockSpec(memory_space=pltpu.VMEM),
        scratch_shapes=[
            pltpu.VMEM((CHUNKS, ROWS, LOCAL // CHUNKS), jnp.bfloat16),
            pltpu.VMEM((512, 128), jnp.int32),
            pltpu.VMEM((64, 128), jnp.int32),
            pltpu.VMEM((64, 128), jnp.int32),
            pltpu.SMEM((64, 128), jnp.int32),
            pltpu.VMEM((128 * STRIDE, 128), jnp.float32),
            pltpu.VMEM((32768, 128), jnp.float32),
            pltpu.VMEM((2, 256, 128), jnp.float32),
            pltpu.VMEM((4096, 128), jnp.float32),
            pltpu.VMEM((4096, 128), jnp.float32),
            pltpu.VMEM((256, 256), jnp.bfloat16),
            pltpu.VMEM((128, 128), jnp.bfloat16),
            pltpu.SemaphoreType.DMA((CHUNKS,)),
            pltpu.SemaphoreType.DMA((3,)),
        ],
        compiler_params=pltpu.CompilerParams(vmem_limit_bytes=60 * 2**20),
    )(grads, sign_bits.reshape(512, 128), columns.reshape(64, 128))


def per_device(grads, sign_bits, columns):
    terms = local(grads, sign_bits, columns)
    scale = 1.0 / jnp.sqrt(jnp.float32(SKETCH))
    sketch = (lax.psum_scatter(terms, "mp", scatter_dimension=0, tiled=True) * scale).astype(jnp.bfloat16)
    everyone = lax.all_gather(sketch, "dp", axis=0, tiled=False)
    partial_gram = jnp.einsum(
        "khn,zkhe->nze",
        sketch.reshape(256, 2, ROWS),
        everyone.reshape(16, 256, 2, ROWS),
        preferred_element_type=jnp.float32,
    ).reshape(ROWS, 16 * ROWS)
    return lax.psum_scatter(partial_gram, "mp", scatter_dimension=1, tiled=True)


def solution(mesh):
    return jax.shard_map(
        per_device,
        mesh=mesh,
        in_specs=(P("dp", "mp"), P("mp"), P()),
        out_specs=P("dp", "mp"),
        check_vma=False,
    )
```

time: 349 us -> 271 us (0.78)
  local copies, waits for them, and re-layouts: 72.5 us -> 4.47 us
  Pallas kernels: 0 us -> 27.2 us
  other arithmetic: 14.3 us -> 1.53 us
  matrix products: 13.5 us -> 1.21 us
  waiting for transfers between devices: 232 us -> 221 us
    gather x1 -> x0, local copies, waits for them, and re-layouts: 38.3 us -> none  [per_device(): terms = flat[:, low] * weight[None, :]]
    pallas_call x0 -> x1, Pallas kernels: none -> 27.2 us  [local(): pl.pallas_call(local_kernel, out_shape=jax.ShapeDtypeStruct((4096, 128),...]
    reshape x1 -> x0, local copies, waits for them, and re-layouts: 23.1 us -> none  [per_device(): flat = second.reshape(rows_here, block_len)]
    mul x2 -> x0, other arithmetic: 12.2 us -> none  [the longest x1 7.98 us: per_device(): signed = (grads * signs[None, :]).reshape(rows_here, size_a, size_b)]
    dot_general x1, matrix products: 11 us -> 1.21 us  [per_device(): jnp.einsum('khn,zkhe->nze', sketch.reshape(256, 2, ROWS), everyone.reshap...]
    reduce_scatter x1, waiting for transfers between devices: 88.7 us -> 79.1 us  [per_device(): lax.psum_scatter(terms, 'mp', scatter_dimension=0, tiled=True) * scale]
    unnamed x4 -> x2, local copies, waits for them, and re-layouts: 10.3 us -> 1.7 us
where the time goes in v1:
time: 271 us; the launch traced here: 269 us
  waiting for transfers between devices  221 us (82%)
  Pallas kernels  27.2 us (10%)
  between operations  13.1 us (5%)
  local copies, waits for them, and re-layouts  4.47 us (2%)
    unnamed x4, waiting for transfers between devices  82.9 us
    reduce_scatter x1, waiting for transfers between devices, per_device(): lax.psum_scatter(terms, 'mp', scatter_dimension=0, tiled=True) * scale  79.1 us
    all_gather x1, waiting for transfers between devices, per_device(): everyone = lax.all_gather(sketch, 'dp', axis=0, tiled=False)  59.2 us
    pallas_call x1, Pallas kernels, local(): pl.pallas_call(local_kernel, out_shape=jax.ShapeDtypeStruct((4096, 128),...  27.2 us
  transfers between devices with their start and end apart: 3, of which 3 were waited for; matrix products, arithmetic and copies ran while one was open for 0% of the time, Pallas kernels for 0%

profile of v1, /device:TPU:7, one launch (start us, length us, event | category | flops | bytes accessed | tf_op | source)
XLA Modules:
  0.0 268.7 jit_solution(13406970222776323917)
XLA Ops:
  6.5 0.0 reduce-scatter.5.cloned.1.call-start
  6.5 27.2 %shard_map.37 = f32[4096,128]{1,0:T(8,128)} custom-call(bf16[64,65536]{1,0:T(8,128)(2,1)} %grads.1, s32[512,128]{1,0:T(8,128)} %bitcast.23, s32[64,128]{1,0:T(8,128)} %bitcast.24), custom_call_target="tpu_custom_call" | custom-call | tf_op jit(solution)/shard_map/pallas_call | solution.py:122
  33.7 0.0 reduce-scatter.5.cloned.1.call-update
  33.7 0.0 all-gather.3.cloned.1.call-start
  33.8 79.1 %reduce-scatter.5.cloned.1.call-done = f32[256,128]{1,0:T(8,128)} async-done(((f32[4096,128]{1,0:T(8,128)}), f32[256,128]{1,0:T(8,128)}) %reduce-scatter.5.cloned.1.call-update) | async-done | bytes 131088 | tf_op jit(solution)/shard_map/reduce_scatter | solution.py:150
  112.9 1.5 multiply_convert_fusion
  114.4 0.0 all-gather.3.cloned.1.call-update
  114.4 0.0 reduce-scatter.7.cloned.1.call-start
  114.5 0.9 copy.9
  115.4 59.2 %all-gather.3.cloned.1.call-done = bf16[4096,128]{1,0:T(8,128)(2,1)} async-done(((bf16[256,128]{1,0:T(8,128)(2,1)}), bf16[4096,128]{1,0:T(8,128)(2,1)}) %all-gather.3.cloned.1.call-update) | async-done | bytes 1048592 | tf_op jit(solution)/shard_map/all_gather | solution.py:151
  174.6 1.5 copy.10
  176.1 0.2 copy.14
  176.3 0.3 copy.11
  176.7 1.2 convolution_bitcast_fusion
  177.9 0.0 reduce-scatter.7.cloned.1.call-update
  177.9 82.9 %reduce-scatter.7.cloned.1.call-done = f32[64,64]{1,0:T(8,128)} async-done(((f32[1024,64]{1,0:T(8,128)}), f32[64,64]{1,0:T(8,128)}) %reduce-scatter.7.cloned.1.call-update) | async-done | bytes 16400
  260.8 1.5 copy.13
Async XLA Ops:
  6.5 106.3 %reduce-scatter.5.cloned.1.call-start = ((), (), s32[]{:S(2)}) async-start(), calls=%async_computation.2 | async-start | bytes 2228224 | tf_op jit(solution)/shard_map/reduce_scatter | solution.py:150
  33.7 140.8 %all-gather.3.cloned.1.call-start = ((), (), s32[]{:S(2)}) async-start(), calls=%async_computation.3 | async-start | bytes 1114112 | tf_op jit(solution)/shard_map/all_gather | solution.py:151
  114.4 146.3 %reduce-scatter.7.cloned.1.call-start = ((), (), s32[]{:S(2)}) async-start(), calls=%async_computation.4 | async-start | bytes 557056
Sparse Core Ops, SparseCore 0:
  33.9 78.9 reduce-scatter.4
  114.8 59.7 all-gather.2
  179.1 81.6 reduce-scatter.6

commit v2 on v1

--- a/solution.py
+++ b/solution.py
@@ -12,6 +12,8 @@
 LOCAL = 65536
 CHUNKS = 16
 STRIDE = 264
+MESH = pl.DeviceIdType.MESH
+SCALE = 1.0 / SKETCH**0.5
 
 
 def parity(v, bits):
@@ -30,9 +32,37 @@
     return (1 - 2 * parity(both, bits)).astype(jnp.float32).astype(jnp.bfloat16)
 
 
-def local_kernel(
-    grads, bits, columns, out, data, sign, cols, rows_v, rows_s, first, second, picked, sa, sb, had_b, had_a, gsem, ssem
+def kernel(
+    grads, bits, columns, out,
+    data, sign, cols, rows_v, rows_s, first, second, picked, sa, sb, had_b, had_a,
+    pair_out, pair_in, own, sum_out, sum_in, ring, beside, left_t, block_out, block_in,
+    gsem, ssem, pair_send, pair_recv, sum_send, sum_recv, right_send, left_send, ring_recv, x_send, x_recv, block_send, block_recv,
 ):
+    me = lax.axis_index("mp")
+    dp = lax.axis_index("dp")
+    core, chip = lax.rem(me, 2), me // 2
+    x, z = lax.rem(dp, 2), dp // 2
+    right, left = lax.rem(z + 1, 8), lax.rem(z + 7, 8)
+    alone = x == core
+
+    barrier = pltpu.get_barrier_semaphore()
+
+    def greet(d, m):
+        pl.semaphore_signal(barrier, inc=1, device_id=(d, m), device_id_type=MESH)
+
+    greet(dp, 2 * chip + 1 - core)
+    for o in range(1, 8):
+        greet(dp, 2 * lax.rem(chip + o, 8) + core)
+    greet(2 * z + 1 - x, me)
+    greet(2 * left + x, me)
+    greet(2 * right + x, me)
+
+    @pl.loop(0, 16)
+    def _(q):
+        @pl.when(jnp.logical_not(jnp.logical_and(alone, q == me)))
+        def _():
+            greet(2 * z + core, q)
+
     copy_sign = pltpu.make_async_copy(bits, sign, ssem.at[0])
     copy_cols = pltpu.make_async_copy(columns, cols, ssem.at[1])
     copy_cols.start()
@@ -51,7 +81,6 @@
     rows_v[...] = ((cv & 255) << 7) | ((cv & 65535) >> 9)
     copy_rows = pltpu.make_async_copy(rows_v, rows_s, ssem.at[2])
     copy_rows.start()
-    me = lax.axis_index("mp")
     eye = iota((128, 128), 0) == iota((128, 128), 1)
     halves = ((iota((256, 128), 0) >> 7) == (iota((256, 128), 1) >> 6)).astype(jnp.float32).astype(jnp.bfloat16)
     w = 1.0 - 2.0 * parity((cv >> 16) & me, 4).astype(jnp.float32)
@@ -77,8 +106,8 @@
             for a in range(4):
                 both = []
                 for h in range(2):
-                    x = data[i, :, pl.ds((q * 4 + a) * 256 + h * 128, 128)]
-                    both.append(x * s[2 * a + h : 2 * a + h + 1, :])
+                    v = data[i, :, pl.ds((q * 4 + a) * 256 + h * 128, 128)]
+                    both.append(v * s[2 * a + h : 2 * a + h + 1, :])
                 parts.append(jnp.concatenate(both, axis=1))
             block = jnp.concatenate(parts, axis=0)
             o = lax.dot_general(had_b[...], block, (((1,), (1,)), ((), ())), preferred_element_type=jnp.float32)
@@ -98,8 +127,7 @@
 
     copy_rows.wait()
 
-    @pl.loop(0, 16)
-    def _(j):
+    def gather(j, dst, at_chip):
         @pl.loop(0, 2)
         def _(u):
             for h in range(2):
@@ -110,52 +138,211 @@
                         picked[h, pl.ds(u * 128 + b * 16 + e, 1), :] = got[e]
 
         low = iota((256, 128), 1) < 64
-        x = picked[0]
-        y = picked[1]
+        p = picked[0]
+        q = picked[1]
         here = pl.ds(pl.multiple_of(j * 256, 256), 256)
-        out[here, :] = (
-            jnp.where(low, x, y) * sa[here, :] + pltpu.roll(jnp.where(low, y, x), 64, 1) * sb[here, :]
-        )
-
-
-def local(grads, sign_bits, columns):
+        dst[at_chip] = (
+            jnp.where(low, p, q) * sa[here, :] + pltpu.roll(jnp.where(low, q, p), 64, 1) * sb[here, :]
+        )
+
+    def to_pair(t):
+        return pltpu.make_async_remote_copy(
+            pair_out.at[t], pair_in.at[t], pair_send.at[t], pair_recv.at[t],
+            device_id=(dp, 2 * chip + 1 - core), device_id_type=MESH,
+        )
+
+    def to_chip(t, slot):
+        return pltpu.make_async_remote_copy(
+            sum_out.at[t], sum_in.at[slot], sum_send.at[t], sum_recv.at[slot],
+            device_id=(dp, 2 * t + core), device_id_type=MESH,
+        )
+
+    @pl.when(alone)
+    def _():
+        pl.semaphore_wait(barrier, 26)
+
+    @pl.when(jnp.logical_not(alone))
+    def _():
+        pl.semaphore_wait(barrier, 27)
+
+    @pl.loop(0, 9)
+    def _(s):
+        @pl.when(s < 8)
+        def _():
+            t = lax.rem(chip + 1 + s, 8)
+            gather(2 * t + 1 - core, pair_out, t)
+            to_pair(t).start()
+            gather(2 * t + core, own, t)
+
+        @pl.when(s > 0)
+        def _():
+            t = lax.rem(chip + s, 8)
+            to_pair(t).wait_recv()
+
+            @pl.when(s < 8)
+            def _():
+                sum_out[t] = (own[t] + pair_in[t]).astype(jnp.bfloat16)
+                to_chip(t, chip).start()
+
+    total = own[chip] + pair_in[chip]
+    for o in range(1, 8):
+        t = lax.rem(chip + o, 8)
+        to_chip(t, t).wait_recv()
+        total += sum_in[t].astype(jnp.float32)
+    ring[z] = (total * SCALE).astype(jnp.bfloat16)
+
+    def to_right(k):
+        slot = lax.rem(z + 8 - k, 8)
+        return pltpu.make_async_remote_copy(
+            ring.at[slot], ring.at[slot], right_send.at[k], ring_recv.at[slot],
+            device_id=(2 * right + x, me), device_id_type=MESH,
+        )
+
+    def to_left(k):
+        slot = lax.rem(z + k, 8)
+        return pltpu.make_async_remote_copy(
+            ring.at[slot], ring.at[slot], left_send.at[k], ring_recv.at[slot],
+            device_id=(2 * left + x, me), device_id_type=MESH,
+        )
+
+    def arrived(slot):
+        pltpu.make_async_remote_copy(
+            ring.at[slot], ring.at[slot], right_send.at[0], ring_recv.at[slot],
+            device_id=(2 * right + x, me), device_id_type=MESH,
+        ).wait_recv()
+
+    to_x = pltpu.make_async_remote_copy(
+        ring.at[z], beside, x_send, x_recv, device_id=(2 * z + 1 - x, me), device_id_type=MESH
+    )
+    to_x.start()
+    to_right(0).start()
+    to_left(0).start()
+
+    def to_owner(k, d, m, slot):
+        return pltpu.make_async_remote_copy(
+            block_out.at[k], block_in.at[slot], block_send.at[k], block_recv.at[slot],
+            device_id=(d, m), device_id_type=MESH,
+        )
+
+    def products(slot):
+        p = jnp.dot(left_t[...], ring[slot], preferred_element_type=jnp.float32)
+        low = iota((32, 128), 1) < 64
+        for rel in range(2):
+            lo, hi = p[rel * 128 : rel * 128 + 64], p[rel * 128 + 64 : rel * 128 + 128]
+            a0, b0, a1, b1 = lo[:32], lo[32:], hi[:32], hi[32:]
+            both = jnp.where(low, a0, b1) + pltpu.roll(jnp.where(low, b0, a1), 64, 1)
+            if rel == 0:
+                mine = jnp.logical_and(alone, slot == chip)
+
+                @pl.when(mine)
+                def _():
+                    block_in[me] = both
+
+                @pl.when(jnp.logical_not(mine))
+                def _():
+                    block_out[2 * slot] = both
+                    to_owner(2 * slot, dp, 2 * slot + x, me).start()
+
+            else:
+                block_out[2 * slot + 1] = both
+                to_owner(2 * slot + 1, 2 * z + 1 - x, 2 * slot + x, me).start()
+
+    left_t[pl.ds(0, 128), :] = ring[z].astype(jnp.float32).T.astype(jnp.bfloat16)
+    to_x.wait_recv()
+    left_t[pl.ds(128, 128), :] = beside[...].astype(jnp.float32).T.astype(jnp.bfloat16)
+    products(z)
+    for k in range(1, 5):
+        down, up = lax.rem(z + 8 - k, 8), lax.rem(z + k, 8)
+        arrived(down)
+        if k < 4:
+            to_right(k).start()
+            arrived(up)
+        if k < 3:
+            to_left(k).start()
+        products(down)
+        if k < 4:
+            products(up)
+
+    @pl.loop(0, 16)
+    def _(q):
+        @pl.when(jnp.logical_not(jnp.logical_and(alone, q == me)))
+        def _():
+            to_owner(0, dp, me, q).wait_recv()
+
+    result = block_in[0]
+    for q in range(1, 16):
+        result += block_in[q]
+    out[pl.ds(0, 32), :] = result[:, :64]
+    out[pl.ds(32, 32), :] = result[:, 64:]
+
+    for t in range(8):
+        to_pair(t).wait_send()
+    for o in range(1, 8):
+        to_chip(lax.rem(chip + o, 8), chip).wait_send()
+    to_x.wait_send()
+    for k in range(4):
+        to_right(k).wait_send()
+    for k in range(3):
+        to_left(k).wait_send()
+
+    @pl.loop(0, 8)
+    def _(slot):
+        to_owner(2 * slot + 1, dp, me, me).wait_send()
+
+        @pl.when(jnp.logical_not(jnp.logical_and(alone, slot == chip)))
+        def _():
+            to_owner(2 * slot, dp, me, me).wait_send()
+
+
+def per_device(grads, sign_bits, columns):
+    f32, bf16 = jnp.float32, jnp.bfloat16
+    dma = pltpu.SemaphoreType.DMA
     return pl.pallas_call(
-        local_kernel,
-        out_shape=jax.ShapeDtypeStruct((4096, 128), jnp.float32),
+        kernel,
+        out_shape=jax.ShapeDtypeStruct((ROWS, ROWS), f32),
         in_specs=[pl.BlockSpec(memory_space=pl.ANY)] * 3,
         out_specs=pl.BlockSpec(memory_space=pltpu.VMEM),
         scratch_shapes=[
-            pltpu.VMEM((CHUNKS, ROWS, LOCAL // CHUNKS), jnp.bfloat16),
+            pltpu.VMEM((CHUNKS, ROWS, LOCAL // CHUNKS), bf16),
             pltpu.VMEM((512, 128), jnp.int32),
             pltpu.VMEM((64, 128), jnp.int32),
             pltpu.VMEM((64, 128), jnp.int32),
             pltpu.SMEM((64, 128), jnp.int32),
-            pltpu.VMEM((128 * STRIDE, 128), jnp.float32),
-            pltpu.VMEM((32768, 128), jnp.float32),
-            pltpu.VMEM((2, 256, 128), jnp.float32),
-            pltpu.VMEM((4096, 128), jnp.float32),
-            pltpu.VMEM((4096, 128), jnp.float32),
-            pltpu.VMEM((256, 256), jnp.bfloat16),
-            pltpu.VMEM((128, 128), jnp.bfloat16),
-            pltpu.SemaphoreType.DMA((CHUNKS,)),
-            pltpu.SemaphoreType.DMA((3,)),
+            pltpu.VMEM((128 * STRIDE, 128), f32),
+            pltpu.VMEM((32768, 128), f32),
+            pltpu.VMEM((2, 256, 128), f32),
+            pltpu.VMEM((4096, 128), f32),
+            pltpu.VMEM((4096, 128), f32),
+            pltpu.VMEM((256, 256), bf16),
+            pltpu.VMEM((128, 128), bf16),
+            pltpu.VMEM((8, 256, 128), f32),
+            pltpu.VMEM((8, 256, 128), f32),
+            pltpu.VMEM((8, 256, 128), f32),
+            pltpu.VMEM((8, 256, 128), bf16),
+            pltpu.VMEM((8, 256, 128), bf16),
+            pltpu.VMEM((8, 256, 128), bf16),
+            pltpu.VMEM((256, 128), bf16),
+            pltpu.VMEM((256, 256), bf16),
+            pltpu.VMEM((16, 32, 128), f32),
+            pltpu.VMEM((16, 32, 128), f32),
+            dma((CHUNKS,)),
+            dma((3,)),
+            dma((8,)),
+            dma((8,)),
+            dma((8,)),
+            dma((8,)),
+            dma((4,)),
+            dma((3,)),
+            dma((8,)),
+            dma,
+            dma,
+            dma((16,)),
+            dma((16,)),
         ],
-        compiler_params=pltpu.CompilerParams(vmem_limit_bytes=60 * 2**20),
+        compiler_params=pltpu.CompilerParams(
+            vmem_limit_bytes=60 * 2**20, collective_id=0, has_side_effects=True
+        ),
     )(grads, sign_bits.reshape(512, 128), columns.reshape(64, 128))
-
-
-def per_device(grads, sign_bits, columns):
-    terms = local(grads, sign_bits, columns)
-    scale = 1.0 / jnp.sqrt(jnp.float32(SKETCH))
-    sketch = (lax.psum_scatter(terms, "mp", scatter_dimension=0, tiled=True) * scale).astype(jnp.bfloat16)
-    everyone = lax.all_gather(sketch, "dp", axis=0, tiled=False)
-    partial_gram = jnp.einsum(
-        "khn,zkhe->nze",
-        sketch.reshape(256, 2, ROWS),
-        everyone.reshape(16, 256, 2, ROWS),
-        preferred_element_type=jnp.float32,
-    ).reshape(ROWS, 16 * ROWS)
-    return lax.psum_scatter(partial_gram, "mp", scatter_dimension=1, tiled=True)
 
 
 def solution(mesh):

time: 271 us -> 60.5 us (0.22)
  waiting for transfers between devices: 221 us -> 0 us
  Pallas kernels: 27.2 us -> 59 us
  between operations: 13.1 us -> 0.01 us
  local copies, waits for them, and re-layouts: 4.47 us -> 1.38 us
    unnamed x4 -> x0, waiting for transfers between devices: 82.9 us -> none
    reduce_scatter x1 -> x0, waiting for transfers between devices: 79.1 us -> none  [per_device(): lax.psum_scatter(terms, 'mp', scatter_dimension=0, tiled=True) * scale]
    all_gather x1 -> x0, waiting for transfers between devices: 59.2 us -> none  [per_device(): everyone = lax.all_gather(sketch, 'dp', axis=0, tiled=False)]
    pallas_call x1, Pallas kernels: 27.2 us -> 59 us  [per_device(): pl.pallas_call(kernel, out_shape=jax.ShapeDtypeStruct((ROWS, ROWS), f32),...]
  transfers between devices with their start and end apart: 3 -> 0, of which waited for: 3 -> 0; matrix products, arithmetic and copies ran while one was open for 0% -> 0% of each run, Pallas kernels for 0% -> 0%
where the time goes in v2:
time: 60.5 us; the launch traced here: 60.4 us
  Pallas kernels  59 us (98%)
  local copies, waits for them, and re-layouts  1.38 us (2%)
    pallas_call x1, Pallas kernels, per_device(): pl.pallas_call(kernel, out_shape=jax.ShapeDtypeStruct((ROWS, ROWS), f32),...  59 us
    unnamed x1, local copies, waits for them, and re-layouts  1.38 us

profile of v2, /device:TPU:7, one launch (start us, length us, event | category | flops | bytes accessed | tf_op | source)
XLA Modules:
  0.0 60.4 jit_solution(6464932034611124187)
XLA Ops:
  0.0 59.0 %shard_map.37 = f32[64,64]{1,0:T(8,128)} custom-call(bf16[64,65536]{1,0:T(8,128)(2,1)} %grads.1, s32[512,128]{1,0:T(8,128)} %bitcast.2, s32[64,128]{1,0:T(8,128)} %bitcast.3), custom_call_target="tpu_custom_call" | custom-call | tf_op jit(solution)/shard_map/pallas_call | solution.py:300
  59.0 1.4 %copy.5 = f32[64,64]{1,0:T(8,128)} copy(f32[64,64]{1,0:T(8,128)} %shard_map.37) | data formatting | bytes 32768

commit v3 on v2

--- a/solution.py
+++ b/solution.py
@@ -10,8 +10,8 @@
 SKETCH = 8192
 ROWS = 64
 LOCAL = 65536
-CHUNKS = 16
-STRIDE = 264
+CHUNKS = 2
+STRIDE = 265
 MESH = pl.DeviceIdType.MESH
 SCALE = 1.0 / SKETCH**0.5
 
@@ -36,15 +36,25 @@
     grads, bits, columns, out,
     data, sign, cols, rows_v, rows_s, first, second, picked, sa, sb, had_b, had_a,
     pair_out, pair_in, own, sum_out, sum_in, ring, beside, left_t, block_out, block_in,
-    gsem, ssem, pair_send, pair_recv, sum_send, sum_recv, right_send, left_send, ring_recv, x_send, x_recv, block_send, block_recv,
+    gsem, ssem, pair_send, pair_recv, sum_send, sum_recv, ring_send, ring_recv, half_recv, x_send, x_recv, block_send, block_recv,
 ):
     me = lax.axis_index("mp")
     dp = lax.axis_index("dp")
     core, chip = lax.rem(me, 2), me // 2
     x, z = lax.rem(dp, 2), dp // 2
-    right, left = lax.rem(z + 1, 8), lax.rem(z + 7, 8)
     alone = x == core
 
+    copy_sign = pltpu.make_async_copy(bits, sign, ssem.at[0])
+    copy_cols = pltpu.make_async_copy(columns, cols, ssem.at[1])
+    copy_cols.start()
+    copy_sign.start()
+    width = LOCAL // CHUNKS
+
+    def chunk(i):
+        return pltpu.make_async_copy(grads.at[:, pl.ds(i * width, width)], data.at[i], gsem.at[i])
+
+    for i in range(CHUNKS):
+        chunk(i).start()
     barrier = pltpu.get_barrier_semaphore()
 
     def greet(d, m):
@@ -54,8 +64,8 @@
     for o in range(1, 8):
         greet(dp, 2 * lax.rem(chip + o, 8) + core)
     greet(2 * z + 1 - x, me)
-    greet(2 * left + x, me)
-    greet(2 * right + x, me)
+    for o in (1, 2, 6, 7):
+        greet(2 * lax.rem(z + o, 8) + x, me)
 
     @pl.loop(0, 16)
     def _(q):
@@ -63,24 +73,18 @@
         def _():
             greet(2 * z + core, q)
 
-    copy_sign = pltpu.make_async_copy(bits, sign, ssem.at[0])
-    copy_cols = pltpu.make_async_copy(columns, cols, ssem.at[1])
-    copy_cols.start()
-    copy_sign.start()
-    width = LOCAL // CHUNKS
-
-    def chunk(i):
-        return pltpu.make_async_copy(grads.at[:, pl.ds(i * width, width)], data.at[i], gsem.at[i])
-
-    for i in range(CHUNKS):
-        chunk(i).start()
     had_b[...] = hadamard(256, 8)
     had_a[...] = hadamard(128, 7)
     copy_cols.wait()
     cv = cols[...]
-    rows_v[...] = ((cv & 255) << 7) | ((cv & 65535) >> 9)
-    copy_rows = pltpu.make_async_copy(rows_v, rows_s, ssem.at[2])
-    copy_rows.start()
+    at_rows = (((cv & 255) << 7) | ((cv & 65535) >> 9)).reshape(8, 8, 128)
+    rows_v[...] = jnp.where(core == 1, at_rows, pltpu.roll(at_rows, 4, 1))
+
+    def window(s, w):
+        return pltpu.make_async_copy(rows_v.at[lax.rem(chip + 1 + s, 8)], rows_s.at[w], ssem.at[2 + w])
+
+    window(0, 0).start()
+    window(1, 1).start()
     eye = iota((128, 128), 0) == iota((128, 128), 1)
     halves = ((iota((256, 128), 0) >> 7) == (iota((256, 128), 1) >> 6)).astype(jnp.float32).astype(jnp.bfloat16)
     w = 1.0 - 2.0 * parity((cv >> 16) & me, 4).astype(jnp.float32)
@@ -100,8 +104,8 @@
     @pl.loop(0, CHUNKS)
     def _(i):
         chunk(i).wait()
-        for q in range(4):
-            s = (2 * sign[pl.ds(pl.multiple_of(i * 32 + q * 8, 8), 8), :] - 1).astype(jnp.float32).astype(jnp.bfloat16)
+        for q in range(64 // CHUNKS):
+            s = (2 * sign[pl.ds(pl.multiple_of(i * (512 // CHUNKS) + q * 8, 8), 8), :] - 1).astype(jnp.float32).astype(jnp.bfloat16)
             parts = []
             for a in range(4):
                 both = []
@@ -111,39 +115,38 @@
                 parts.append(jnp.concatenate(both, axis=1))
             block = jnp.concatenate(parts, axis=0)
             o = lax.dot_general(had_b[...], block, (((1,), (1,)), ((), ())), preferred_element_type=jnp.float32)
-            g = pl.multiple_of((i * 4 + q) * (2 * STRIDE), 8)
+            g = (i * (64 // CHUNKS) + q) * (2 * STRIDE)
             first[pl.ds(g, 256), :] = o[:, :128]
-            first[pl.ds(pl.multiple_of(g + STRIDE, 8), 256), :] = o[:, 128:]
-
-    @pl.loop(0, 32)
+            first[pl.ds(g + STRIDE, 256), :] = o[:, 128:]
+
+    @pl.loop(0, 4)
     def _(i):
-        for q in range(4):
-            c = i * 8 + q * 2
+        for q in range(32):
+            c = (i * 32 + q) * 2
             z0 = first[pl.ds(c, 128, stride=STRIDE), :].astype(jnp.bfloat16)
             z1 = first[pl.ds(c + 1, 128, stride=STRIDE), :].astype(jnp.bfloat16)
             o = jnp.dot(had_a[...], jnp.concatenate([z0, z1], axis=1), preferred_element_type=jnp.float32)
             second[pl.ds(pl.multiple_of(c * 128, 128), 128), :] = o[:, :128]
             second[pl.ds(pl.multiple_of(c * 128 + 128, 128), 128), :] = o[:, 128:]
 
-    copy_rows.wait()
-
-    def gather(j, dst, at_chip):
-        @pl.loop(0, 2)
-        def _(u):
+    low = iota((128, 128), 1) < 64
+
+    def gather(w, which, j, dst, at_chip):
+        for u in range(2):
             for h in range(2):
+                spot = (which * 2 + u) * 2 + h
                 for b in range(8):
-                    at = [rows_s[j * 4 + u + 2 * h, b * 16 + e] for e in range(16)]
+                    at = [rows_s[w, which * 4 + 2 * h + u, b * 16 + e] for e in range(16)]
                     got = [second[pl.ds(r, 1), :] for r in at]
                     for e in range(16):
-                        picked[h, pl.ds(u * 128 + b * 16 + e, 1), :] = got[e]
-
-        low = iota((256, 128), 1) < 64
-        p = picked[0]
-        q = picked[1]
-        here = pl.ds(pl.multiple_of(j * 256, 256), 256)
-        dst[at_chip] = (
-            jnp.where(low, p, q) * sa[here, :] + pltpu.roll(jnp.where(low, q, p), 64, 1) * sb[here, :]
-        )
+                        picked[spot, pl.ds(b * 16 + e, 1), :] = got[e]
+        for u in range(2):
+            p = picked[(which * 2 + u) * 2]
+            q = picked[(which * 2 + u) * 2 + 1]
+            here = pl.ds(pl.multiple_of(j * 256 + u * 128, 128), 128)
+            dst[at_chip, pl.ds(u * 128, 128), :] = (
+                jnp.where(low, p, q) * sa[here, :] + pltpu.roll(jnp.where(low, q, p), 64, 1) * sb[here, :]
+            )
 
     def to_pair(t):
         return pltpu.make_async_remote_copy(
@@ -159,31 +162,40 @@
 
     @pl.when(alone)
     def _():
-        pl.semaphore_wait(barrier, 26)
+        pl.semaphore_wait(barrier, 28)
 
     @pl.when(jnp.logical_not(alone))
     def _():
-        pl.semaphore_wait(barrier, 27)
-
-    @pl.loop(0, 9)
-    def _(s):
-        @pl.when(s < 8)
-        def _():
+        pl.semaphore_wait(barrier, 29)
+
+    def add_pair(t):
+        to_pair(t).wait_recv()
+        sum_out[t] = (own[t] + pair_in[t]).astype(jnp.bfloat16)
+        to_chip(t, chip).start()
+
+    @pl.loop(0, 4)
+    def _(i):
+        for w in range(2):
+            s = 2 * i + w
             t = lax.rem(chip + 1 + s, 8)
-            gather(2 * t + 1 - core, pair_out, t)
+            window(s, w).wait()
+            gather(w, 0, 2 * t + 1 - core, pair_out, t)
             to_pair(t).start()
-            gather(2 * t + core, own, t)
-
-        @pl.when(s > 0)
-        def _():
-            t = lax.rem(chip + s, 8)
-            to_pair(t).wait_recv()
-
-            @pl.when(s < 8)
+            gather(w, 1, 2 * t + core, own, t)
+
+            @pl.when(i < 3)
             def _():
-                sum_out[t] = (own[t] + pair_in[t]).astype(jnp.bfloat16)
-                to_chip(t, chip).start()
-
+                window(s + 2, w).start()
+
+            if w == 1:
+                add_pair(lax.rem(chip + s, 8))
+            else:
+
+                @pl.when(i > 0)
+                def _():
+                    add_pair(lax.rem(chip + s, 8))
+
+    to_pair(chip).wait_recv()
     total = own[chip] + pair_in[chip]
     for o in range(1, 8):
         t = lax.rem(chip + o, 8)
@@ -191,32 +203,26 @@
         total += sum_in[t].astype(jnp.float32)
     ring[z] = (total * SCALE).astype(jnp.bfloat16)
 
-    def to_right(k):
-        slot = lax.rem(z + 8 - k, 8)
+    def along(n, slot, part, sem):
+        here = ring.at[slot, pl.ds(0, 256)] if part is None else ring.at[slot, pl.ds(part * 128, 128)]
+        got = half_recv if part == 1 else ring_recv.at[slot]
         return pltpu.make_async_remote_copy(
-            ring.at[slot], ring.at[slot], right_send.at[k], ring_recv.at[slot],
-            device_id=(2 * right + x, me), device_id_type=MESH,
+            here, here, ring_send.at[sem], got, device_id=(2 * lax.rem(z + n, 8) + x, me), device_id_type=MESH
         )
 
-    def to_left(k):
-        slot = lax.rem(z + k, 8)
-        return pltpu.make_async_remote_copy(
-            ring.at[slot], ring.at[slot], left_send.at[k], ring_recv.at[slot],
-            device_id=(2 * left + x, me), device_id_type=MESH,
-        )
-
     def arrived(slot):
-        pltpu.make_async_remote_copy(
-            ring.at[slot], ring.at[slot], right_send.at[0], ring_recv.at[slot],
-            device_id=(2 * right + x, me), device_id_type=MESH,
-        ).wait_recv()
+        along(1, slot, None, 0).wait_recv()
+
+    def at(n):
+        return lax.rem(z + n, 8)
 
     to_x = pltpu.make_async_remote_copy(
         ring.at[z], beside, x_send, x_recv, device_id=(2 * z + 1 - x, me), device_id_type=MESH
     )
+    sent = [along(2, z, None, 0), along(6, z, None, 1), along(1, z, None, 2), along(7, z, None, 3)]
     to_x.start()
-    to_right(0).start()
-    to_left(0).start()
+    for copy in sent:
+        copy.start()
 
     def to_owner(k, d, m, slot):
         return pltpu.make_async_remote_copy(
@@ -251,17 +257,22 @@
     to_x.wait_recv()
     left_t[pl.ds(128, 128), :] = beside[...].astype(jnp.float32).T.astype(jnp.bfloat16)
     products(z)
-    for k in range(1, 5):
-        down, up = lax.rem(z + 8 - k, 8), lax.rem(z + k, 8)
-        arrived(down)
-        if k < 4:
-            to_right(k).start()
-            arrived(up)
-        if k < 3:
-            to_left(k).start()
-        products(down)
-        if k < 4:
-            products(up)
+    for n, back, part in ((6, 1, 0), (2, 7, 1)):
+        arrived(at(n))
+        sent += [along(back, at(n), None, 4 + 2 * part), along(8 - n, at(n), part, 5 + 2 * part)]
+        sent[-2].start()
+        sent[-1].start()
+    for n in (7, 1):
+        arrived(at(n))
+        products(at(n))
+    products(at(6))
+    products(at(2))
+    for n in (5, 3):
+        arrived(at(n))
+        products(at(n))
+    along(2, at(4), 0, 0).wait_recv()
+    along(6, at(4), 1, 0).wait_recv()
+    products(at(4))
 
     @pl.loop(0, 16)
     def _(q):
@@ -280,10 +291,8 @@
     for o in range(1, 8):
         to_chip(lax.rem(chip + o, 8), chip).wait_send()
     to_x.wait_send()
-    for k in range(4):
-        to_right(k).wait_send()
-    for k in range(3):
-        to_left(k).wait_send()
+    for copy in sent:
+        copy.wait_send()
 
     @pl.loop(0, 8)
     def _(slot):
@@ -306,11 +315,11 @@
             pltpu.VMEM((CHUNKS, ROWS, LOCAL // CHUNKS), bf16),
             pltpu.VMEM((512, 128), jnp.int32),
             pltpu.VMEM((64, 128), jnp.int32),
-            pltpu.VMEM((64, 128), jnp.int32),
-            pltpu.SMEM((64, 128), jnp.int32),
+            pltpu.VMEM((8, 8, 128), jnp.int32),
+            pltpu.SMEM((2, 8, 128), jnp.int32),
             pltpu.VMEM((128 * STRIDE, 128), f32),
             pltpu.VMEM((32768, 128), f32),
-            pltpu.VMEM((2, 256, 128), f32),
+            pltpu.VMEM((8, 128, 128), f32),
             pltpu.VMEM((4096, 128), f32),
             pltpu.VMEM((4096, 128), f32),
             pltpu.VMEM((256, 256), bf16),
@@ -326,14 +335,14 @@
             pltpu.VMEM((16, 32, 128), f32),
             pltpu.VMEM((16, 32, 128), f32),
             dma((CHUNKS,)),
-            dma((3,)),
-            dma((8,)),
-            dma((8,)),
-            dma((8,)),
-            dma((8,)),
             dma((4,)),
-            dma((3,)),
-            dma((8,)),
+            dma((8,)),
+            dma((8,)),
+            dma((8,)),
+            dma((8,)),
+            dma((8,)),
+            dma((8,)),
+            dma,
             dma,
             dma,
             dma((16,)),

time: 60.5 us -> 44.6 us (0.74)
  Pallas kernels: 59 us -> 42.7 us
    pallas_call x1, Pallas kernels: 59 us -> 42.7 us  [per_device(): pl.pallas_call(kernel, out_shape=jax.ShapeDtypeStruct((ROWS, ROWS), f32),...]
where the time goes in v3:
time: 44.6 us; the launch traced here: 44.1 us
  Pallas kernels  42.7 us (96%)
  local copies, waits for them, and re-layouts  1.38 us (3%)
    pallas_call x1, Pallas kernels, per_device(): pl.pallas_call(kernel, out_shape=jax.ShapeDtypeStruct((ROWS, ROWS), f32),...  42.7 us
    unnamed x1, local copies, waits for them, and re-layouts  1.38 us

profile of v3, /device:TPU:7, one launch (start us, length us, event | category | flops | bytes accessed | tf_op | source)
XLA Modules:
  0.0 44.1 jit_solution(13961094385112605724)
XLA Ops:
  0.0 42.7 %shard_map.37 = f32[64,64]{1,0:T(8,128)} custom-call(bf16[64,65536]{1,0:T(8,128)(2,1)} %grads.1, s32[512,128]{1,0:T(8,128)} %bitcast.2, s32[64,128]{1,0:T(8,128)} %bitcast.3), custom_call_target="tpu_custom_call" | custom-call | tf_op jit(solution)/shard_map/pallas_call | solution.py:309
  42.7 1.4 %copy.5 = f32[64,64]{1,0:T(8,128)} copy(f32[64,64]{1,0:T(8,128)} %shard_map.37) | data formatting | bytes 32768

commit v4 on v3

--- a/solution.py
+++ b/solution.py
@@ -36,7 +36,7 @@
     grads, bits, columns, out,
     data, sign, cols, rows_v, rows_s, first, second, picked, sa, sb, had_b, had_a,
     pair_out, pair_in, own, sum_out, sum_in, ring, beside, left_t, block_out, block_in,
-    gsem, ssem, pair_send, pair_recv, sum_send, sum_recv, ring_send, ring_recv, half_recv, x_send, x_recv, block_send, block_recv,
+    gsem, ssem, pair_send, pair_recv, sum_send, sum_recv, ring_send, ring_recv, x_send, x_recv, block_send, block_recv,
 ):
     me = lax.axis_index("mp")
     dp = lax.axis_index("dp")
@@ -80,11 +80,17 @@
     at_rows = (((cv & 255) << 7) | ((cv & 65535) >> 9)).reshape(8, 8, 128)
     rows_v[...] = jnp.where(core == 1, at_rows, pltpu.roll(at_rows, 4, 1))
 
-    def window(s, w):
-        return pltpu.make_async_copy(rows_v.at[lax.rem(chip + 1 + s, 8)], rows_s.at[w], ssem.at[2 + w])
+    across, y = chip // 4, lax.rem(chip, 4)
+
+    def served(i, w):
+        dx = 1 - (i + 2 * w) // 3
+        return 4 * lax.rem(across + dx, 2) + lax.rem(y + 2 - w + i, 4)
+
+    def window(i, w):
+        return pltpu.make_async_copy(rows_v.at[served(i, w)], rows_s.at[w], ssem.at[2 + w])
 
     window(0, 0).start()
-    window(1, 1).start()
+    window(0, 1).start()
     eye = iota((128, 128), 0) == iota((128, 128), 1)
     halves = ((iota((256, 128), 0) >> 7) == (iota((256, 128), 1) >> 6)).astype(jnp.float32).astype(jnp.bfloat16)
     w = 1.0 - 2.0 * parity((cv >> 16) & me, 4).astype(jnp.float32)
@@ -131,7 +137,7 @@
 
     low = iota((128, 128), 1) < 64
 
-    def gather(w, which, j, dst, at_chip):
+    def gather(w, which):
         for u in range(2):
             for h in range(2):
                 spot = (which * 2 + u) * 2 + h
@@ -140,6 +146,8 @@
                     got = [second[pl.ds(r, 1), :] for r in at]
                     for e in range(16):
                         picked[spot, pl.ds(b * 16 + e, 1), :] = got[e]
+
+    def combine(which, j, dst, at_chip):
         for u in range(2):
             p = picked[(which * 2 + u) * 2]
             q = picked[(which * 2 + u) * 2 + 1]
@@ -173,45 +181,67 @@
         sum_out[t] = (own[t] + pair_in[t]).astype(jnp.bfloat16)
         to_chip(t, chip).start()
 
+    window(0, 0).wait()
+    gather(0, 0)
+
     @pl.loop(0, 4)
     def _(i):
         for w in range(2):
-            s = 2 * i + w
-            t = lax.rem(chip + 1 + s, 8)
-            window(s, w).wait()
-            gather(w, 0, 2 * t + 1 - core, pair_out, t)
+            t = served(i, w)
+            gather(w, 1)
+            combine(0, 2 * t + 1 - core, pair_out, t)
             to_pair(t).start()
-            gather(w, 1, 2 * t + core, own, t)
 
             @pl.when(i < 3)
             def _():
-                window(s + 2, w).start()
-
-            if w == 1:
-                add_pair(lax.rem(chip + s, 8))
+                window(i + 1, w).start()
+
+            if w == 0:
+                window(i, 1).wait()
+                gather(1, 0)
+                combine(1, 2 * t + core, own, t)
+
+                @pl.when(i > 0)
+                def _():
+                    add_pair(served(i - 1, 1))
+
             else:
 
-                @pl.when(i > 0)
-                def _():
-                    add_pair(lax.rem(chip + s, 8))
+                @pl.when(i < 3)
+                def _():
+                    window(i + 1, 0).wait()
+                    gather(0, 0)
+                    combine(1, 2 * t + core, own, t)
+                    add_pair(served(i, 0))
+
+                @pl.when(i == 3)
+                def _():
+                    add_pair(served(i, 0))
+                    combine(1, 2 * t + core, own, t)
 
     to_pair(chip).wait_recv()
     total = own[chip] + pair_in[chip]
-    for o in range(1, 8):
-        t = lax.rem(chip + o, 8)
+    for n in range(7):
+        t = served(n // 2, n % 2)
         to_chip(t, t).wait_recv()
         total += sum_in[t].astype(jnp.float32)
     ring[z] = (total * SCALE).astype(jnp.bfloat16)
 
     def along(n, slot, part, sem):
-        here = ring.at[slot, pl.ds(0, 256)] if part is None else ring.at[slot, pl.ds(part * 128, 128)]
-        got = half_recv if part == 1 else ring_recv.at[slot]
+        here = ring.at[slot, pl.ds(part * 128, 128)]
         return pltpu.make_async_remote_copy(
-            here, here, ring_send.at[sem], got, device_id=(2 * lax.rem(z + n, 8) + x, me), device_id_type=MESH
+            here, here, ring_send.at[sem], ring_recv.at[slot, part],
+            device_id=(2 * lax.rem(z + n, 8) + x, me), device_id_type=MESH,
         )
 
-    def arrived(slot):
-        along(1, slot, None, 0).wait_recv()
+    sent = []
+
+    def pass_on(n, slot, part):
+        sent.append(along(n, slot, part, len(sent)))
+        sent[-1].start()
+
+    def arrived(slot, part):
+        along(1, slot, part, 0).wait_recv()
 
     def at(n):
         return lax.rem(z + n, 8)
@@ -219,10 +249,13 @@
     to_x = pltpu.make_async_remote_copy(
         ring.at[z], beside, x_send, x_recv, device_id=(2 * z + 1 - x, me), device_id_type=MESH
     )
-    sent = [along(2, z, None, 0), along(6, z, None, 1), along(1, z, None, 2), along(7, z, None, 3)]
+    for part in range(2):
+        pass_on(2, z, part)
+        pass_on(6, z, 1 - part)
     to_x.start()
-    for copy in sent:
-        copy.start()
+    for part in range(2):
+        pass_on(1, z, part)
+        pass_on(7, z, part)
 
     def to_owner(k, d, m, slot):
         return pltpu.make_async_remote_copy(
@@ -257,18 +290,18 @@
     to_x.wait_recv()
     left_t[pl.ds(128, 128), :] = beside[...].astype(jnp.float32).T.astype(jnp.bfloat16)
     products(z)
-    for n, back, part in ((6, 1, 0), (2, 7, 1)):
-        arrived(at(n))
-        sent += [along(back, at(n), None, 4 + 2 * part), along(8 - n, at(n), part, 5 + 2 * part)]
-        sent[-2].start()
-        sent[-1].start()
-    for n in (7, 1):
-        arrived(at(n))
-        products(at(n))
+    for n, part in ((6, 0), (2, 1)):
+        arrived(at(n), part)
+        pass_on(8 - n, at(n), part)
+        pass_on(1 if n == 6 else 7, at(n), part)
+    for n, part in ((6, 1), (2, 0)):
+        arrived(at(n), part)
+        pass_on(1 if n == 6 else 7, at(n), part)
     products(at(6))
     products(at(2))
-    for n in (5, 3):
-        arrived(at(n))
+    for n in (7, 1, 5, 3):
+        arrived(at(n), 0)
+        arrived(at(n), 1)
         products(at(n))
     along(2, at(4), 0, 0).wait_recv()
     along(6, at(4), 1, 0).wait_recv()
@@ -340,9 +373,8 @@
             dma((8,)),
             dma((8,)),
             dma((8,)),
-            dma((8,)),
-            dma((8,)),
-            dma,
+            dma((14,)),
+            dma((8, 2)),
             dma,
             dma,
             dma((16,)),

time: 44.6 us -> 42.6 us (0.955)
  Pallas kernels: 42.7 us -> 41.1 us
    pallas_call x1, Pallas kernels: 42.7 us -> 41.1 us  [per_device(): pl.pallas_call(kernel, out_shape=jax.ShapeDtypeStruct((ROWS, ROWS), f32),...]
where the time goes in v4:
time: 42.6 us; the launch traced here: 42.4 us
  Pallas kernels  41.1 us (96%)
  local copies, waits for them, and re-layouts  1.38 us (3%)
    pallas_call x1, Pallas kernels, per_device(): pl.pallas_call(kernel, out_shape=jax.ShapeDtypeStruct((ROWS, ROWS), f32),...  41.1 us
    unnamed x1, local copies, waits for them, and re-layouts  1.38 us

profile of v4, /device:TPU:7, one launch (start us, length us, event | category | flops | bytes accessed | tf_op | source)
XLA Modules:
  0.0 42.4 jit_solution(16499767696154958608)
XLA Ops:
  0.0 41.1 %shard_map.37 = f32[64,64]{1,0:T(8,128)} custom-call(bf16[64,65536]{1,0:T(8,128)(2,1)} %grads.1, s32[512,128]{1,0:T(8,128)} %bitcast.2, s32[64,128]{1,0:T(8,128)} %bitcast.3), custom_call_target="tpu_custom_call" | custom-call | tf_op jit(solution)/shard_map/pallas_call | solution.py:342
  41.1 1.4 %copy.5 = f32[64,64]{1,0:T(8,128)} copy(f32[64,64]{1,0:T(8,128)} %shard_map.37) | data formatting | bytes 32768

commit v5 on v4

--- a/solution.py
+++ b/solution.py
@@ -78,7 +78,9 @@
     copy_cols.wait()
     cv = cols[...]
     at_rows = (((cv & 255) << 7) | ((cv & 65535) >> 9)).reshape(8, 8, 128)
-    rows_v[...] = jnp.where(core == 1, at_rows, pltpu.roll(at_rows, 4, 1))
+    turned = pltpu.roll(at_rows, 4, 1)
+    rows_v[0] = jnp.where(core == 1, at_rows, turned)
+    rows_v[1] = jnp.where(core == 1, turned, at_rows)
 
     across, y = chip // 4, lax.rem(chip, 4)
 
@@ -86,11 +88,14 @@
         dx = 1 - (i + 2 * w) // 3
         return 4 * lax.rem(across + dx, 2) + lax.rem(y + 2 - w + i, 4)
 
-    def window(i, w):
-        return pltpu.make_async_copy(rows_v.at[served(i, w)], rows_s.at[w], ssem.at[2 + w])
-
-    window(0, 0).start()
-    window(0, 1).start()
+    def window(which, i, w):
+        return pltpu.make_async_copy(
+            rows_v.at[which, served(i, w)], rows_s.at[which, w], ssem.at[2 + 2 * which + w]
+        )
+
+    for which in range(2):
+        for w in range(2):
+            window(which, 0, w).start()
     eye = iota((128, 128), 0) == iota((128, 128), 1)
     halves = ((iota((256, 128), 0) >> 7) == (iota((256, 128), 1) >> 6)).astype(jnp.float32).astype(jnp.bfloat16)
     w = 1.0 - 2.0 * parity((cv >> 16) & me, 4).astype(jnp.float32)
@@ -137,12 +142,12 @@
 
     low = iota((128, 128), 1) < 64
 
-    def gather(w, which):
+    def gather(which, w):
         for u in range(2):
             for h in range(2):
                 spot = (which * 2 + u) * 2 + h
                 for b in range(8):
-                    at = [rows_s[w, which * 4 + 2 * h + u, b * 16 + e] for e in range(16)]
+                    at = [rows_s[which, w, 2 * h + u, b * 16 + e] for e in range(16)]
                     got = [second[pl.ds(r, 1), :] for r in at]
                     for e in range(16):
                         picked[spot, pl.ds(b * 16 + e, 1), :] = got[e]
@@ -181,43 +186,58 @@
         sum_out[t] = (own[t] + pair_in[t]).astype(jnp.bfloat16)
         to_chip(t, chip).start()
 
-    window(0, 0).wait()
-    gather(0, 0)
+    def gather_next(i, w, refill):
+        window(0, i, w).wait()
+        gather(0, w)
+        if refill is None:
+            window(0, i + 1, w).start()
+        else:
+
+            @pl.when(refill)
+            def _():
+                window(0, i + 1, w).start()
+
+    def send_pair(i, w):
+        t = served(i, w)
+        combine(0, 2 * t + 1 - core, pair_out, t)
+        to_pair(t).start()
+
+    gather_next(0, 0, None)
+    send_pair(0, 0)
+    gather_next(0, 1, None)
 
     @pl.loop(0, 4)
     def _(i):
         for w in range(2):
             t = served(i, w)
-            gather(w, 1)
-            combine(0, 2 * t + 1 - core, pair_out, t)
-            to_pair(t).start()
+            window(1, i, w).wait()
+            if w == 0:
+                gather(1, 0)
+                send_pair(i, 1)
+            else:
+
+                @pl.when(i < 3)
+                def _():
+                    gather(1, 1)
+                    send_pair(i + 1, 0)
+
+                @pl.when(i == 3)
+                def _():
+                    gather(1, 1)
 
             @pl.when(i < 3)
             def _():
-                window(i + 1, w).start()
-
+                window(1, i + 1, w).start()
+                gather_next(i + 1, w, i < 2)
+
+            combine(1, 2 * t + core, own, t)
             if w == 0:
-                window(i, 1).wait()
-                gather(1, 0)
-                combine(1, 2 * t + core, own, t)
-
-                @pl.when(i > 0)
-                def _():
-                    add_pair(served(i - 1, 1))
-
+                add_pair(t)
             else:
 
                 @pl.when(i < 3)
                 def _():
-                    window(i + 1, 0).wait()
-                    gather(0, 0)
-                    combine(1, 2 * t + core, own, t)
-                    add_pair(served(i, 0))
-
-                @pl.when(i == 3)
-                def _():
-                    add_pair(served(i, 0))
-                    combine(1, 2 * t + core, own, t)
+                    add_pair(t)
 
     to_pair(chip).wait_recv()
     total = own[chip] + pair_in[chip]
@@ -290,19 +310,30 @@
     to_x.wait_recv()
     left_t[pl.ds(128, 128), :] = beside[...].astype(jnp.float32).T.astype(jnp.bfloat16)
     products(z)
-    for n, part in ((6, 0), (2, 1)):
-        arrived(at(n), part)
-        pass_on(8 - n, at(n), part)
-        pass_on(1 if n == 6 else 7, at(n), part)
-    for n, part in ((6, 1), (2, 0)):
-        arrived(at(n), part)
-        pass_on(1 if n == 6 else 7, at(n), part)
-    products(at(6))
-    products(at(2))
-    for n in (7, 1, 5, 3):
+    late = lax.rem(z + 2, 8) // 4
+    one, two, three = 1 + 6 * late, 2 + 4 * late, 3 + 2 * late
+
+    def relay(n, back, part):
+        for last in range(2):
+            half = part + last - 2 * part * last
+            arrived(at(n), half)
+            if last == 0:
+                pass_on(8 - n, at(n), half)
+            pass_on(back, at(n), half)
+
+    def take(n):
         arrived(at(n), 0)
         arrived(at(n), 1)
         products(at(n))
+
+    relay(two, 8 - one, 1 - late)
+    products(at(two))
+    relay(8 - two, one, late)
+    products(at(8 - two))
+    take(one)
+    take(8 - one)
+    take(three)
+    take(8 - three)
     along(2, at(4), 0, 0).wait_recv()
     along(6, at(4), 1, 0).wait_recv()
     products(at(4))
@@ -348,8 +379,8 @@
             pltpu.VMEM((CHUNKS, ROWS, LOCAL // CHUNKS), bf16),
             pltpu.VMEM((512, 128), jnp.int32),
             pltpu.VMEM((64, 128), jnp.int32),
-            pltpu.VMEM((8, 8, 128), jnp.int32),
-            pltpu.SMEM((2, 8, 128), jnp.int32),
+            pltpu.VMEM((2, 8, 8, 128), jnp.int32),
+            pltpu.SMEM((2, 2, 8, 128), jnp.int32),
             pltpu.VMEM((128 * STRIDE, 128), f32),
             pltpu.VMEM((32768, 128), f32),
             pltpu.VMEM((8, 128, 128), f32),
@@ -368,7 +399,7 @@
             pltpu.VMEM((16, 32, 128), f32),
             pltpu.VMEM((16, 32, 128), f32),
             dma((CHUNKS,)),
-            dma((4,)),
+            dma((6,)),
             dma((8,)),
             dma((8,)),
             dma((8,)),

time: 42.6 us -> 42.3 us (level)
  no operation moved by 1% of the time
where the time goes in v5:
time: 42.3 us; the launch traced here: 42.1 us
  Pallas kernels  40.8 us (96%)
  local copies, waits for them, and re-layouts  1.38 us (3%)
    pallas_call x1, Pallas kernels, per_device(): pl.pallas_call(kernel, out_shape=jax.ShapeDtypeStruct((ROWS, ROWS), f32),...  40.8 us
    unnamed x1, local copies, waits for them, and re-layouts  1.38 us

profile of v5, /device:TPU:7, one launch (start us, length us, event | category | flops | bytes accessed | tf_op | source)
XLA Modules:
  0.0 42.1 jit_solution(1369995330402302635)
XLA Ops:
  0.0 40.8 %shard_map.37 = f32[64,64]{1,0:T(8,128)} custom-call(bf16[64,65536]{1,0:T(8,128)(2,1)} %grads.1, s32[512,128]{1,0:T(8,128)} %bitcast.2, s32[64,128]{1,0:T(8,128)} %bitcast.3), custom_call_target="tpu_custom_call" | custom-call | tf_op jit(solution)/shard_map/pallas_call | solution.py:373
  40.8 1.4 %copy.5 = f32[64,64]{1,0:T(8,128)} copy(f32[64,64]{1,0:T(8,128)} %shard_map.37) | data formatting | bytes 32768

commit v6 on v5

--- a/solution.py
+++ b/solution.py
@@ -248,9 +248,9 @@
     ring[z] = (total * SCALE).astype(jnp.bfloat16)
 
     def along(n, slot, part, sem):
-        here = ring.at[slot, pl.ds(part * 128, 128)]
+        here = ring.at[slot] if part is None else ring.at[slot, pl.ds(part * 128, 128)]
         return pltpu.make_async_remote_copy(
-            here, here, ring_send.at[sem], ring_recv.at[slot, part],
+            here, here, ring_send.at[sem], ring_recv.at[slot, 0 if part is None else part],
             device_id=(2 * lax.rem(z + n, 8) + x, me), device_id_type=MESH,
         )
 
@@ -273,9 +273,8 @@
         pass_on(2, z, part)
         pass_on(6, z, 1 - part)
     to_x.start()
-    for part in range(2):
-        pass_on(1, z, part)
-        pass_on(7, z, part)
+    pass_on(1, z, None)
+    pass_on(7, z, None)
 
     def to_owner(k, d, m, slot):
         return pltpu.make_async_remote_copy(
@@ -330,8 +329,9 @@
     products(at(two))
     relay(8 - two, one, late)
     products(at(8 - two))
-    take(one)
-    take(8 - one)
+    for n in (one, 8 - one):
+        arrived(at(n), None)
+        products(at(n))
     take(three)
     take(8 - three)
     along(2, at(4), 0, 0).wait_recv()

time: 42.3 us -> 42.3 us (level)
  no operation moved by 1% of the time
where the time goes in v6:
time: 42.3 us; the launch traced here: 42.1 us
  Pallas kernels  40.8 us (96%)
  local copies, waits for them, and re-layouts  1.38 us (3%)
    pallas_call x1, Pallas kernels, per_device(): pl.pallas_call(kernel, out_shape=jax.ShapeDtypeStruct((ROWS, ROWS), f32),...  40.8 us
    unnamed x1, local copies, waits for them, and re-layouts  1.38 us

profile of v6, /device:TPU:7, one launch (start us, length us, event | category | flops | bytes accessed | tf_op | source)
XLA Modules:
  0.0 42.1 jit_solution(14366553451048201687)
XLA Ops:
  0.0 40.8 %shard_map.37 = f32[64,64]{1,0:T(8,128)} custom-call(bf16[64,65536]{1,0:T(8,128)(2,1)} %grads.1, s32[512,128]{1,0:T(8,128)} %bitcast.2, s32[64,128]{1,0:T(8,128)} %bitcast.3), custom_call_target="tpu_custom_call" | custom-call | tf_op jit(solution)/shard_map/pallas_call | solution.py:373
  40.8 1.4 %copy.5 = f32[64,64]{1,0:T(8,128)} copy(f32[64,64]{1,0:T(8,128)} %shard_map.37) | data formatting | bytes 32768
